TPU v7x, 32 devices: a whole 2x2x4 slice. The times are simulated.
32 devices in a mesh: gx: 4 (over y, x), gy: 4 (over z), gz: 2 (over core).
Axes of the slice: x: 2, y: 2, z: 4, core: 2. Of those that a mesh axis runs over, the one named last changes fastest.
Arguments:
- nodal_field: float32 [128, 512, 512], P('gx', 'gy', 'gz'), may hold values from -6 to 6
- spacing_x: float32 [128], replicated, may hold values from 0.5 to 2
- spacing_z: float32 [512], replicated, may hold values from 0.5 to 2
- operator_x: float32 [64, 16], P('gx'), may hold values from -1.5 to 1.5
- persist_x: float32 [64], P('gx'), may hold values from 0.6 to 1
- operator_z: float32 [256, 128], P('gz'), may hold values from -0.5 to 0.5
- persist_z: float32 [256], P('gz'), may hold values from 0.6 to 1
- receivers: int32 [16384, 1], P(('gx', 'gy', 'gz')), may hold values from 0 to 7; in each aligned block of 512 rows (0 to 511, 512 to 1023, ...) at most 128 rows name the same one
Outputs:
- detail_x: float32 [64, 512, 512], P('gx', 'gy', 'gz')
- detail_z: float32 [64, 512, 256], P('gx', 'gy', 'gz')
- received: float32 [32, 8, 128, 2, 4, 128], P(('gx', 'gy', 'gz'))
Inputs may be any that keep to these rules, and one draw needn't show every extreme that they name: `receivers`: each row names the receiving device of one kept block among the 8 devices with the same gx index, in (gy, gz) row-major order; of the 512 blocks of one device at most 128 name the same receiver, and that bound is reached.
All inputs are finite; a program needn't handle non-finite values.
Results may differ from a plain program's by a relative error of at most 0.00008.
Values sent between devices are 32-bit elements; how exact they have to be, the bound alone decides.
A program may use at most 64 MiB of HBM per device.

v0:
```python
import jax
import jax.numpy as jnp
from jax import lax
from jax.sharding import PartitionSpec as P

LINES = 4


def extended(block, sides, width):
    for axis, dim in sides:
        count = lax.axis_size(axis)
        forward = [(i, i + 1) for i in range(count - 1)]
        backward = [(target, source) for source, target in forward]
        low = lax.ppermute(
            lax.slice_in_dim(block, block.shape[dim] - width, None, axis=dim), axis, forward
        )
        high = lax.ppermute(lax.slice_in_dim(block, 0, width, axis=dim), axis, backward)
        block = jnp.concatenate([low, block, high], axis=dim)
    return block


def carried_in(array, axis, combine, identity):
    size, index = (lax.axis_size(axis), lax.axis_index(axis))
    everything = jax.tree.map(lambda part: lax.all_gather(part, axis), array)
    start = jax.tree.map(
        lambda part, zero: jnp.broadcast_to(jnp.asarray(zero, part.dtype), part.shape),
        array,
        identity,
    )

    def step(k, before):
        reached = k < index
        new = combine(before, jax.tree.map(lambda part: part[k], everything))
        return jax.tree.map(lambda a, b: jnp.where(reached, a, b), new, before)

    return lax.fori_loop(0, size, step, start)


def compose(earlier, later):
    return (earlier[0] * later[0], later[1] + later[0] * earlier[1])


def edges_first(border):
    return extended(border, (("gx", 0),), 2)


def edges_third(border):
    return extended(border, (("gz", 2),), 2)


def chain_first(gain_end, value_end):
    identity = (jnp.ones_like(gain_end), jnp.zeros_like(value_end))
    return carried_in((gain_end, value_end), "gx", compose, identity)[1]


def chain_third(gain_end, value_end):
    identity = (jnp.ones_like(gain_end), jnp.zeros_like(value_end))
    return carried_in((gain_end, value_end), "gz", compose, identity)[1]


def expand(vector, direction):
    shape_list = [1, 1, 1]
    shape_list[direction] = -1
    return vector.reshape(shape_list)


def refine(nodes, spacing, row_blocks, gain_list, direction, device_rank, edges_move, chain_move):
    length = nodes.shape[direction]
    coarse_count = length // 2
    offset = device_rank * length
    local_space = lax.dynamic_slice_in_dim(spacing, offset, length)
    prev_space = lax.dynamic_slice_in_dim(spacing, jnp.maximum(offset - 2, 0), 2)
    space_even = local_space[0::2]
    space_odd = local_space[1::2]
    span_sum = space_even + space_odd
    weight_a = space_odd / span_sum
    weight_b = space_even / span_sum
    even_nodes = lax.slice_in_dim(nodes, 0, length, 2, direction)
    odd_nodes = lax.slice_in_dim(nodes, 1, length, 2, direction)
    border = jnp.concatenate(
        [
            lax.slice_in_dim(nodes, 0, 2, axis=direction),
            lax.slice_in_dim(nodes, length - 2, length, axis=direction),
        ],
        direction,
    )
    widened = edges_move(border)
    left_even = lax.slice_in_dim(widened, 0, 1, axis=direction)
    left_odd = lax.slice_in_dim(widened, 1, 2, axis=direction)
    beyond = lax.slice_in_dim(widened, 6, 7, axis=direction)
    right_nodes = jnp.concatenate(
        [lax.slice_in_dim(even_nodes, 1, coarse_count, axis=direction), beyond], direction
    )
    detail = (
        odd_nodes
        - expand(weight_a, direction) * even_nodes
        - expand(weight_b, direction) * right_nodes
    )
    first_even = lax.slice_in_dim(even_nodes, 0, 1, axis=direction)
    prev_sum = prev_space[0] + prev_space[1]
    left_detail = (
        left_odd - prev_space[1] / prev_sum * left_even - prev_space[0] / prev_sum * first_even
    )
    from_left = jnp.where(device_rank > 0, 0.5 * prev_space[1] * left_detail, 0.0)
    near_terms = 0.5 * expand(space_even, direction) * detail
    far_terms = 0.5 * expand(space_odd, direction) * detail
    load_terms = near_terms + jnp.concatenate(
        [from_left, lax.slice_in_dim(far_terms, 0, coarse_count - 1, axis=direction)], direction
    )
    if direction == 0:
        local_part = jnp.einsum(
            "ij,jab->iab", row_blocks, load_terms, precision=lax.Precision.HIGHEST
        )
    else:
        local_part = jnp.einsum(
            "ij,abj->abi", row_blocks, load_terms, precision=lax.Precision.HIGHEST
        )
    tail_values = lax.slice_in_dim(local_part, coarse_count - 1, coarse_count, axis=direction)
    gain_end = gain_list[coarse_count - 1 : coarse_count].reshape(1, 1, 1)
    carried = chain_move(gain_end, tail_values)
    solved = local_part + expand(gain_list, direction) * carried
    return (detail, even_nodes + solved)


def local(
    nodal_field, spacing_x, spacing_z, operator_x, persist_x, operator_z, persist_z, receivers
):
    index_first = lax.axis_index("gx")
    index_third = lax.axis_index("gz")
    detail_x, coarse_x = refine(
        nodal_field, spacing_x, operator_x, persist_x, 0, index_first, edges_first, chain_first
    )
    detail_z, coarse_z = refine(
        coarse_x, spacing_z, operator_z, persist_z, 2, index_third, edges_third, chain_third
    )
    depth_cells = coarse_z.shape[2]
    block_count = coarse_z.shape[0] * coarse_z.shape[1] // LINES
    tile_rows = jnp.stack(
        [
            coarse_z.reshape(block_count, LINES, depth_cells),
            detail_z.reshape(block_count, LINES, depth_cells),
        ],
        1,
    )
    tile_rows = tile_rows.reshape(block_count, 2 * LINES * depth_cells)
    group_size = lax.axis_size("gy") * lax.axis_size("gz")
    capacity = max(2, block_count // group_size * 2)
    targets = receivers[:, 0]
    positions = jnp.arange(block_count, dtype=jnp.int32)
    earlier = (targets[None, :] == targets[:, None]) & (positions[None, :] < positions[:, None])
    slots = jnp.sum(earlier.astype(jnp.int32), axis=1)
    placed = targets * capacity + slots
    selector = (
        placed[None, :] == jnp.arange(group_size * capacity, dtype=jnp.int32)[:, None]
    ).astype(jnp.float32)
    outgoing = jnp.dot(
        selector, tile_rows, precision=lax.Precision.HIGHEST, preferred_element_type=jnp.float32
    )
    outgoing = outgoing.reshape(group_size, capacity, 2 * LINES * depth_cells)
    incoming = lax.all_to_all(outgoing, ("gy", "gz"), split_axis=0, concat_axis=0, tiled=True)
    received = incoming.reshape(1, group_size, capacity, 2, LINES, depth_cells)
    return (detail_x, detail_z, received)


def solution(mesh):
    return jax.shard_map(
        local,
        mesh=mesh,
        in_specs=(
            P("gx", "gy", "gz"),
            P(),
            P(),
            P("gx", None),
            P("gx"),
            P("gz", None),
            P("gz"),
            P(("gx", "gy", "gz"), None),
        ),
        out_specs=(
            P("gx", "gy", "gz"),
            P("gx", "gy", "gz"),
            P(("gx", "gy", "gz"), None, None, None, None, None),
        ),
        check_vma=False,
    )
```

profile of v0, /device:TPU:0, one launch (start us, length us, event | category | flops | bytes accessed | tf_op | source)
XLA Modules:
  0.0 206.3 jit_solution(16318343252056938121)
XLA Ops:
  0.7 1.1 fusion.25
  1.9 1.3 collective-permute-start
  3.4 5.5 %collective-permute-start.1 = (f32[2,128,256]{1,0,2:T(2,128)S(1)}, f32[2,128,256]{1,0,2:T(2,128)S(1)}, u32[]{:S(2)}, u32[]{:S(2)}) collective-permute-start(f32[2,128,256]{1,0,2:T(2,128)S(1)} %copy.111), channel_id=1, source_target_pairs={{0,8},{8,16},{16,24},{1,9},{9,17},{17,25},{2,10},{10,18},{18,26},{... | collective-permute-start | bytes 786440 | tf_op jit(solution)/shard_map/ppermute | solution.py:14
  9.0 0.2 slice.120
  9.2 0.2 slice.119
  9.8 4.0 %fusion.26 = (f32[16,128,256]{2,1,0:T(8,128)S(1)}, f32[16,128,256]{2,1,0:T(8,128)}) fusion(f32[32,128,256]{2,1,0:T(8,128)} %param.12), kind=kLoop, calls=%fused_computation.60 | loop fusion | bytes 8388608 | tf_op jit(solution)/shard_map/slice | solution.py:79
  13.9 0.6 dynamic-slice.1
  14.5 0.7 dynamic-slice
  15.2 0.6 fusion.28
  15.7 0.6 fusion.29
  16.3 0.2 convert_reduce_fusion
  16.6 0.9 slice_dynamic-update-slice_fusion.1
  17.5 0.7 slice_dynamic-update-slice_fusion
  18.2 10.3 %all-reduce = f32[4]{0:T(128)S(1)} all-reduce(f32[4]{0:T(128)S(1)} %slice_dynamic-update-slice_fusion.1), channel_id=3, replica_groups=mesh['gx'=4,'gy'=4,'gz'=2] {'gx'}, use_global_device_ids=true, to_apply=%add | all-reduce | flops 4 | bytes 32
  31.9 2.0 copy.108
  33.8 2.2 %copy.109 = f32[16,128,256]{1,0,2:T(8,128)S(1)} copy(f32[16,128,256]{2,1,0:T(8,128)} %get-tuple-element.317) | data formatting | bytes 4194304
  36.4 1.3 copy-done.6
  37.7 0.6 fusion.1
  38.3 0.2 slice_multiply_fusion
  38.5 0.3 broadcast_select_fusion.2
  38.8 0.8 copy-done.1
  39.6 2.3 %fusion.8 = f32[16,128,256]{1,0,2:T(8,128)S(1)} fusion(f32[15,128,256]{1,0,2:T(8,128)S(1)} %slice_multiply_fusion, f32[1,128,256]{1,0,2:T(1,128)S(1)} %broadcast_select_fusion.2, f32[16,128,256]{1,0,2:T(8,128)S(1)} %fusion.1, f32[16]{0:T(128)S(1)} %get-tuple-element.328, f32[16,16]{1,0:T(8,128)S(1)} %copy-done.11), kind=kOutput, calls=%fused_computation.19 | convolution fusion | flops 102236160 | bytes 6292544 | tf_op jit(solution)/shard_map/ij,jab->iab/dot_general | solution.py:111
  41.9 1.3 copy-done.5
  43.4 10.0 %all-gather = f32[4,128,256]{2,1,0:T(8,128)S(1)} all-gather(f32[1,128,256]{2,1,0:T(8,128)S(1)} %copy.94), channel_id=2, replica_groups=mesh['gx'=4,'gy'=4,'gz'=2] {'gx'}, dimensions={0}, use_global_device_ids=true | all-gather | bytes 655360 | tf_op jit(solution)/shard_map/all_gather | solution.py:24
  53.4 5.0 %while.28 = (s32[]{:T(128)}, f32[1,128,256]{2,1,0:T(8,128)S(1)}, s32[]{:T(128)}, f32[4,1,128,256]{3,2,1,0:T(8,128)S(1)}, f32[4,1,1,1]{0,3,2,1:T(1,128)S(1)}, /*index=5*/s32[]{:T(128)}, s32[]{:T(128)}) while((s32[]{:T(128)}, f32[1,128,256]{2,1,0:T(8,128)S(1)}, s32[]{:T(128)}, f32[4,1,128,256]{3,2,1,0:T(8,128)S(1)}, ...), condition=%wide.region_1.2_spmd.clone, body=%wide.region_0.1_spmd.clone.sunk | while | flops 131076 | bytes 393341 | solution.py:36
  53.4 0.6 constant_dynamic-slice_fusion.6
  54.0 0.6 fusion.32
  54.6 0.6 constant_dynamic-slice_fusion.6
  55.2 0.6 fusion.32
  55.9 0.6 constant_dynamic-slice_fusion.6
  56.5 0.6 fusion.32
  57.1 0.6 constant_dynamic-slice_fusion.6
  57.7 0.6 fusion.32
  58.5 2.0 add_add_fusion
  60.4 1.3 copy-done.3
  61.8 1.3 collective-permute-start.2
  63.1 3.3 %all-reduce.1 = f32[2]{0:T(128)S(1)} all-reduce(f32[2]{0:T(128)S(1)} %slice_dynamic-update-slice_fusion), channel_id=5, replica_groups=mesh['gx'=4,'gy'=4,'gz'=2] {'gz'}, use_global_device_ids=true, to_apply=%add.1 | all-reduce | flops 2 | bytes 16
  69.6 1.5 slice.121
  71.1 2.2 %collective-permute-start.3 = (f32[16,128,2]{1,0,2:T(8,128)S(1)}, f32[16,128,2]{1,0,2:T(8,128)S(1)}, u32[]{:S(2)}, u32[]{:S(2)}) collective-permute-start(f32[16,128,2]{1,0,2:T(8,128)S(1)} %get-tuple-element.318), channel_id=1, source_target_pairs={{0,1},{2,3},{4,5},{6,7},{8,9},{10,11},{12,13},{14,15},{16,17},{18,... | collective-permute-start | bytes 49160 | tf_op jit(solution)/shard_map/ppermute | solution.py:14
  73.5 0.4 fusion.9
  73.8 1.2 slice_multiply_fusion.1
  75.0 1.4 copy.105
  76.4 0.7 fusion.21
  77.1 1.4 maximum_add_fusion.4
  78.5 1.9 fusion.10
  80.4 1.4 copy.100
  81.8 1.3 slice.151
  83.2 1.6 copy.98
  84.8 2.0 all-gather.2
  86.8 2.5 %while.29 = (s32[]{:T(128)}, f32[16,128,1]{1,2,0:T(1,128)S(1)}, s32[]{:T(128)}, f32[2,16,128,1]{2,1,3,0:T(8,128)S(1)}, f32[2,1,1,1]{0,3,2,1:T(1,128)S(1)}, /*index=5*/s32[]{:T(128)}, s32[]{:T(128)}) while((s32[]{:T(128)}, f32[16,128,1]{1,2,0:T(1,128)S(1)}, s32[]{:T(128)}, f32[2,16,128,1]{2,1,3,0:T(8,128)S(1)}, ...), condition=%wide.region_4.5_spmd.clone, body=%wide.region_3.4_spmd.clone.sunk | while | flops 8196 | bytes 41085 | solution.py:36
  86.8 0.6 constant_dynamic-slice_fusion.8
  87.4 0.6 broadcast_select_fusion.4
  88.1 0.6 constant_dynamic-slice_fusion.8
  88.7 0.6 broadcast_select_fusion.4
  89.3 1.2 add_add_fusion.1
  90.5 1.7 copy.101
  92.2 0.5 pad_maximum_fusion
  92.6 1.7 copy.103
  94.3 2.1 %reshape.92 = f32[512,1024,1]{1,0,2:T(8,128)S(1)} reshape(f32[512,2,4,128]{3,2,1,0:T(4,128)} %copy.103) | data formatting | bytes 4194304 | tf_op jit(solution)/shard_map/reshape | solution.py:145
  96.4 5.1 %fusion.6 = f32[8,128,1024]{2,1,0:T(8,128)} fusion(f32[512,1024,1]{1,0,2:T(8,128)S(1)} %reshape.92, s32[8,128]{1,0:T(8,128)S(1)} %multiply_add_fusion, s32[512]{0:T(512)S(1)} %multiply_add_fusion.1), kind=kOutput, calls=%fused_computation.17 | convolution fusion | flops 6442975232 | bytes 6297600 | tf_op jit(solution)/shard_map/dot_general | solution.py:156
  101.6 5.0 %all-to-all-start = ((f32[8,128,1024]{2,1,0:T(8,128)}), f32[8,128,1024]{2,1,0:T(8,128)}, u32[]{:S(2)}, u32[]{:S(2)}) async-start(f32[8,128,1024]{2,1,0:T(8,128)} %fusion.6), calls=%async_computation | async-start | bytes 8388608 | tf_op jit(solution)/shard_map/all_to_all | solution.py:160
  106.6 1.8 copy.104
  108.4 92.3 %all-to-all-done = f32[8,128,1024]{2,1,0:T(8,128)} async-done(((f32[8,128,1024]{2,1,0:T(8,128)}), f32[8,128,1024]{2,1,0:T(8,128)}, u32[]{:S(2)}, u32[]{:S(2)}) %all-to-all-start) | async-done | bytes 4194336 | tf_op jit(solution)/shard_map/all_to_all | solution.py:160
  200.7 5.6 %reshape.75 = f32[1,8,128,2,4,128]{5,4,3,2,1,0:T(4,128)} reshape(f32[8,128,1024]{2,1,0:T(8,128)} %all-to-all-done) | data formatting | bytes 8388608 | tf_op jit(solution)/shard_map/reshape | solution.py:161
  (62 shorter events, 1.6 us)
Async XLA Ops:
  0.6 77.9 %copy-start = (f32[128,128]{1,0:T(8,128)S(1)}, f32[128,128]{1,0:T(8,128)}, u32[]{:S(2)}) copy-start(f32[128,128]{1,0:T(8,128)} %param.17) | copy-start | bytes 196612
  0.6 8.2 %copy-start.13 = (f32[512]{0:T(512)S(1)}, f32[512]{0:T(512)}, u32[]{:S(2)}) copy-start(f32[512]{0:T(512)} %param.14) | copy-start | bytes 6148
  0.7 8.8 %copy-start.15 = (f32[128]{0:T(128)S(1)}, f32[128]{0:T(128)}, u32[]{:S(2)}) copy-start(f32[128]{0:T(128)} %param.13) | copy-start | bytes 1540
  1.9 34.4 %collective-permute-start = (f32[2,128,256]{1,0,2:T(2,128)S(1)}, f32[2,128,256]{1,0,2:T(2,128)S(1)}, u32[]{:S(2)}, u32[]{:S(2)}) collective-permute-start(f32[2,128,256]{1,0,2:T(2,128)S(1)} %copy.110), channel_id=1, source_target_pairs={{8,0},{16,8},{24,16},{9,1},{17,9},{25,17},{10,2},{18,10},{26,18},{... | collective-permute-start | bytes 786440 | tf_op jit(solution)/shard_map/ppermute | solution.py:17
  3.4 35.1 %collective-permute-start.1 = (f32[2,128,256]{1,0,2:T(2,128)S(1)}, f32[2,128,256]{1,0,2:T(2,128)S(1)}, u32[]{:S(2)}, u32[]{:S(2)}) collective-permute-start(f32[2,128,256]{1,0,2:T(2,128)S(1)} %copy.111), channel_id=1, source_target_pairs={{0,8},{8,16},{16,24},{1,9},{9,17},{17,25},{2,10},{10,18},{18,26},{... | collective-permute-start | bytes 786440 | tf_op jit(solution)/shard_map/ppermute | solution.py:14
  9.7 4.2 %copy-start.17 = (u32[32]{0:T(128)S(1)}, u32[32]{0:T(128)}, u32[]{:S(2)}) copy-start(u32[32]{0:T(128)} %constant.86) | copy-start | bytes 388
  9.7 4.8 %copy-start.16 = (u32[32]{0:T(128)S(1)}, u32[32]{0:T(128)}, u32[]{:S(2)}) copy-start(u32[32]{0:T(128)} %constant.81) | copy-start | bytes 388
  9.7 6.6 %copy-start.10 = (s32[512,1]{0,1:T(1,128)S(1)}, s32[512,1]{0,1:T(1,128)}, u32[]{:S(2)}) copy-start(s32[512,1]{0,1:T(1,128)} %param.19) | copy-start | bytes 6148
  9.8 6.9 %copy-start.12 = (f32[16]{0:T(128)S(1)}, f32[16]{0:T(128)}, u32[]{:S(2)}) copy-start(f32[16]{0:T(128)} %param.16) | copy-start | bytes 196
  9.8 7.7 %copy-start.14 = (f32[128]{0:T(128)S(1)}, f32[128]{0:T(128)}, u32[]{:S(2)}) copy-start(f32[128]{0:T(128)} %param.18) | copy-start | bytes 1540
  36.1 1.6 copy-start.6
  38.3 1.3 copy-start.1
  38.3 1.3 copy-start.11
  41.9 1.3 copy-start.5
  60.4 1.3 copy-start.3
  61.8 11.7 %collective-permute-start.2 = (f32[16,128,2]{1,0,2:T(8,128)S(1)}, f32[16,128,2]{1,0,2:T(8,128)S(1)}, u32[]{:S(2)}, u32[]{:S(2)}) collective-permute-start(f32[16,128,2]{1,0,2:T(8,128)S(1)} %get-tuple-element.319), channel_id=1, source_target_pairs={{1,0},{3,2},{5,4},{7,6},{9,8},{11,10},{13,12},{15,14},{17,16},{19,... | collective-permute-start | bytes 49160 | tf_op jit(solution)/shard_map/ppermute | solution.py:17
  69.6 3.9 %copy-start.4 = (f32[16,128,256]{1,0,2:T(8,128)S(1)}, f32[16,128,256]{1,0,2:T(8,128)}, u32[]{:S(2)}) copy-start(f32[16,128,256]{1,0,2:T(8,128)} %copy-done.3) | copy-start | bytes 6291460
  71.1 2.4 %copy-start.8 = (f32[16,128,128]{1,0,2:T(8,128)}, f32[16,128,128]{1,0,2:T(8,128)S(1)}, u32[]{:S(2)}) copy-start(f32[16,128,128]{1,0,2:T(8,128)S(1)} %slice.121) | copy-start | bytes 3145732
  71.1 5.3 %collective-permute-start.3 = (f32[16,128,2]{1,0,2:T(8,128)S(1)}, f32[16,128,2]{1,0,2:T(8,128)S(1)}, u32[]{:S(2)}, u32[]{:S(2)}) collective-permute-start(f32[16,128,2]{1,0,2:T(8,128)S(1)} %get-tuple-element.318), channel_id=1, source_target_pairs={{0,1},{2,3},{4,5},{6,7},{8,9},{10,11},{12,13},{14,15},{16,17},{18,... | collective-permute-start | bytes 49160 | tf_op jit(solution)/shard_map/ppermute | solution.py:14
  83.2 6.2 %copy-start.7 = (f32[16,128,128]{1,0,2:T(8,128)S(1)}, f32[16,128,128]{1,0,2:T(8,128)}, u32[]{:S(2)}) copy-start(f32[16,128,128]{1,0,2:T(8,128)} %copy.100) | copy-start | bytes 3145732
  90.5 1.7 copy-start.9
  101.5 5.0 %copy-start.2 = (f32[16,128,256]{1,0,2:T(8,128)S(1)}, f32[16,128,256]{1,0,2:T(8,128)}, u32[]{:S(2)}) copy-start(f32[16,128,256]{1,0,2:T(8,128)} %copy-done.1) | copy-start | bytes 6291460
  101.6 99.1 %all-to-all-start = ((f32[8,128,1024]{2,1,0:T(8,128)}), f32[8,128,1024]{2,1,0:T(8,128)}, u32[]{:S(2)}, u32[]{:S(2)}) async-start(f32[8,128,1024]{2,1,0:T(8,128)} %fusion.6), calls=%async_computation | async-start | bytes 8388608 | tf_op jit(solution)/shard_map/all_to_all | solution.py:160
where the time goes:
time: 207 us; the launch traced here: 206 us
  waiting for transfers between devices  92.3 us (45%)
  local copies, waits for them, and re-layouts  43.6 us (21%)
  blocking collectives  25.6 us (12%)
  starting transfers between devices  15.3 us (7%)
  other arithmetic  12.4 us (6%)
  matrix products  9.31 us (4%)
  between operations  7.69 us (4%)
    all_to_all x1, waiting for transfers between devices, local(): lax.all_to_all(outgoing, ('gy', 'gz'), split_axis=0, concat_axis=0, tiled...  92.3 us
    unnamed x48, local copies, waits for them, and re-layouts  15.3 us
    unnamed x2, blocking collectives  13.6 us
    all_gather x2, blocking collectives, carried_in(): everything = jax.tree.map(lambda part: lax.all_gather(part, axis), array)  12 us
    ppermute x2, starting transfers between devices, extended(): lax.ppermute(lax.slice_in_dim(block, block.shape[dim] - width, None, axis...  7.73 us
    reshape x1, local copies, waits for them, and re-layouts, local(): received = incoming.reshape(1, group_size, capacity, 2, LINES, depth_cells)  5.61 us
    dot_general x1, matrix products, local(): jnp.dot(selector, tile_rows, precision=lax.Precision.HIGHEST, preferred_e...  5.13 us
    all_to_all x1, starting transfers between devices, local(): lax.all_to_all(outgoing, ('gy', 'gz'), split_axis=0, concat_axis=0, tiled...  5.01 us
  transfers between devices with their start and end apart: 5, of which 1 were waited for; matrix products, arithmetic and copies ran while one was open for 10% of the time, Pallas kernels for 0%

commit v1 on v0

v1 whole, which is shorter than its diff:
```python
import functools

import jax
import jax.numpy as jnp
from jax import lax
from jax.experimental import pallas as pl
from jax.experimental.pallas import tpu as pltpu
from jax.sharding import PartitionSpec as P

LINES = 4
MESH = pl.DeviceIdType.MESH
HIGHEST = lax.Precision.HIGHEST
LIMIT = 40 * 1024 * 1024


def coefficients(spacing):
    pairs = spacing.reshape(-1, 2)
    even, odd = pairs[:, 0], pairs[:, 1]
    total = even + odd
    a, b = odd / total, even / total

    def before(row):
        return jnp.concatenate([jnp.zeros_like(row[:1]), row[:-1]])

    zero = jnp.zeros_like(a)
    return jnp.stack(
        [a, b, 0.5 * even, before(0.5 * odd), before(a), before(b), zero, zero]
    )


def exchange_first(count, nodes, coefs, factor, gain, out, left, right, send, tails, sems):
    me = lax.axis_index("gx")
    half = nodes.shape[0] // 2
    lines = nodes.shape[1]
    total = count * half
    send_sem, recv_sem = sems
    barrier = pltpu.get_barrier_semaphore()
    for d in range(1, count):
        pl.semaphore_signal(
            barrier, inc=1, device_id={"gx": lax.rem(me + d, count)}, device_id_type=MESH
        )

    def coef(row, k):
        return coefs[row * total + me * half + k]

    last = half - 1
    send[1, pl.ds(0, lines), :] = nodes[2 * last + 1] - coef(0, last) * nodes[2 * last]
    pl.semaphore_wait(barrier, count - 1)

    to_right = pltpu.make_async_remote_copy(
        src_ref=send.at[1, pl.ds(0, lines)], dst_ref=left, send_sem=send_sem.at[0], recv_sem=recv_sem.at[0],
        device_id={"gx": lax.rem(me + 1, count)}, device_id_type=MESH,
    )
    to_left = pltpu.make_async_remote_copy(
        src_ref=nodes.at[0], dst_ref=right, send_sem=send_sem.at[1], recv_sem=recv_sem.at[1],
        device_id={"gx": lax.rem(me + count - 1, count)}, device_id_type=MESH,
    )

    @pl.when(me < count - 1)
    def _():
        to_right.start()

    @pl.when(me > 0)
    def _():
        to_left.start()

    weights = []
    for k in range(half):
        weight = factor[last, k] * coef(2, k)
        if k < last:
            weight = weight + factor[last, k + 1] * coef(3, k + 1)
        weights.append(weight)
    edge = factor[last, 0] * coef(3, 0)

    def chunk(i, carry):
        rows = pl.ds(pl.multiple_of(i * 8, 8), 8)
        even = nodes[0, rows, :]
        value = (-edge * coef(5, 0)) * even
        for k in range(half):
            detail = nodes[2 * k + 1, rows, :] - coef(0, k) * even
            if k < last:
                even = nodes[2 * k + 2, rows, :]
                detail = detail - coef(1, k) * even
            value = value + weights[k] * detail
        send[0, rows, :] = value
        return carry

    lax.fori_loop(0, lines // 8, chunk, 0)

    @pl.when(me == 0)
    def _():
        left[...] = jnp.zeros_like(left)

    @pl.when(me == count - 1)
    def _():
        right[...] = jnp.zeros_like(right)

    @pl.when(me > 0)
    def _():
        to_right.wait_recv()

    @pl.when(me < count - 1)
    def _():
        to_left.wait_recv()

    end = -(factor[last, last] * coef(2, last)) * coef(1, last)
    own = send.at[0]
    own[pl.ds(0, lines), :] = own[pl.ds(0, lines), :] + edge * left[...] + end * right[...]
    own[pl.ds(lines, 8), :] = jnp.full((8, own.shape[1]), gain[last], jnp.float32)

    copies = []
    for d in range(1, count):
        copies.append(
            pltpu.make_async_remote_copy(
                src_ref=tails.at[0], dst_ref=tails.at[d],
                send_sem=send_sem.at[1 + d], recv_sem=recv_sem.at[1 + d],
                device_id={"gx": lax.rem(me + d, count)}, device_id_type=MESH,
            )
        )
    tails[0] = own[...]
    for d in range(1, count):

        @pl.when(me + d < count)
        def _(d=d):
            copies[d - 1].start()

    out[0] = left[...]
    out[1] = right[...]
    out[2] = jnp.zeros_like(left)
    for d in range(count - 1, 0, -1):

        @pl.when(me >= d)
        def _(d=d):
            copies[d - 1].wait_recv()
            out[2] = (
                tails[d, pl.ds(0, lines), :]
                + jnp.max(tails[d, pl.ds(lines, 8), :], axis=0, keepdims=True) * out[2]
            )

    @pl.when(me < count - 1)
    def _():
        to_right.wait_send()

    @pl.when(me > 0)
    def _():
        to_left.wait_send()

    for d in range(1, count):

        @pl.when(me + d < count)
        def _(d=d):
            copies[d - 1].wait_send()


def loads(coefz):
    width = coefz.shape[1]
    row = lax.broadcasted_iota(jnp.int32, (2 * width, width), 0)
    twice = 2 * lax.broadcasted_iota(jnp.int32, (2 * width, width), 1)
    a, b, half_even, half_odd, a_before, b_before = [coefz[k : k + 1, :] for k in range(6)]
    zero = jnp.zeros((2 * width, width), jnp.float32)
    detail = jnp.where(row == twice, -a, zero)
    detail = jnp.where(row == twice + 1, 1.0, detail)
    detail = jnp.where(row == twice + 2, -b, detail)
    earlier = jnp.where(row == twice - 2, -a_before, zero)
    earlier = jnp.where(row == twice - 1, 1.0, earlier)
    earlier = jnp.where(row == twice, -b_before, earlier)
    return detail, half_even * detail + half_odd * earlier, row == twice


def first_kernel(
    nodes, planes, coefs, factor, gain, coefz, factor_z, gain_z, detail, coarse, payload,
    weights, *, count,
):
    me = lax.axis_index("gx")
    half = detail.shape[0]
    total = count * half

    def coef(row, k):
        return coefs[row * total + me * half + k]

    width = factor_z.shape[0]

    @pl.when(pl.program_id(0) == 0)
    def _():
        load = loads(coefz)[1]
        tail = lax.dot_general(
            factor_z[pl.ds(width - 8, 8), :], load, (((1,), (1,)), ((), ())), precision=HIGHEST
        )
        lane = lax.broadcasted_iota(jnp.int32, (1, 2 * width), 1)
        a_last = coefz[0:1, width - 1 : width]
        weights[...] = jnp.zeros_like(weights)
        weights[0:1, :] = jnp.where(lane == 0, 1.0, 0.0)
        weights[1:2, :] = jnp.where(
            lane == 2 * width - 2, -a_last, jnp.where(lane == 2 * width - 1, 1.0, 0.0)
        )
        weights[2:3, :] = tail[7:8, :]

    for i in range(nodes.shape[1] // 8):
        rows = pl.ds(i * 8, 8)
        even = [nodes[2 * k, rows, :] for k in range(half)]
        before = planes[0, rows, :] - coef(5, 0) * even[0]
        load = []
        for k in range(half):
            after = even[k + 1] if k + 1 < half else planes[1, rows, :]
            value = nodes[2 * k + 1, rows, :] - coef(0, k) * even[k] - coef(1, k) * after
            detail[k, rows, :] = value
            load.append(coef(2, k) * value + coef(3, k) * before)
            before = value
        for k in range(half):
            value = nodes[2 * k, rows, :] + gain[k] * planes[2, rows, :]
            for j in range(half):
                value = value + factor[k, j] * load[j]
            coarse[k, rows, :] = value

    lines = coarse[...].reshape(half * coarse.shape[1], coarse.shape[2])
    sent = lax.dot_general(
        weights[...], lines, (((1,), (1,)), ((), ())), precision=HIGHEST
    )
    kind = lax.broadcasted_iota(jnp.int32, sent.shape, 0)
    end_gain = gain_z[0:1, width - 1 : width]
    end_first = factor_z[width - 1 : width, 0:1] * coefz[3:4, 0:1]
    end_last = -(
        factor_z[width - 1 : width, width - 1 : width]
        * coefz[2:3, width - 1 : width]
        * coefz[1:2, width - 1 : width]
    )
    sent = jnp.where(kind == 3, end_gain, sent)
    sent = jnp.where(kind == 4, end_first, sent)
    sent = jnp.where(kind == 5, end_last, sent)
    payload[0] = sent


def third_kernel(
    placed, coarse, gathered, coefz, factor_z, gain_z, detail, outgoing, matrix, update, tiles,
    *, count, chunks,
):
    me = lax.axis_index("gz")
    step = pl.program_id(0)
    width = factor_z.shape[0]

    @pl.when(step == 0)
    def _():
        outgoing[...] = jnp.zeros_like(outgoing)
        detail_of, load_of, is_even = loads(coefz)
        solved = lax.dot_general(
            load_of, factor_z[...], (((1,), (1,)), ((), ())), precision=HIGHEST
        )
        matrix[:, 0:width] = jnp.where(is_even, 1.0, 0.0) + solved
        matrix[:, width:] = detail_of
        turned = factor_z[...].T
        b_last = coefz[1:2, width - 1 : width]
        lane = lax.broadcasted_iota(jnp.int32, (1, width), 1)
        update[...] = jnp.zeros_like(update)
        update[0:1, 0:width] = -turned[width - 1 : width, :] * (
            coefz[2:3, width - 1 : width] * b_last
        )
        update[0:1, width:] = jnp.where(lane == width - 1, -b_last, 0.0)
        update[1:2, 0:width] = turned[0:1, :] * coefz[3:4, 0:1]
        update[2:3, 0:width] = gain_z[...]

    def heard(p, row):
        return gathered[p, 0, row : row + 1, :]

    empty = jnp.zeros_like(heard(0, 0))
    right, left, carry = empty, empty, empty
    for p in range(count):
        right = jnp.where(me + 1 == p, heard(p, 0), right)
        left = jnp.where(me - 1 == p, heard(p, 1), left)
        if p < count - 1:
            tail = heard(p, 2) + heard(p, 5) * heard(p + 1, 0) + heard(p, 3) * carry
            if p > 0:
                tail = tail + heard(p, 4) * heard(p - 1, 1)
            carry = jnp.where(p < me, tail, carry)
    kind = lax.broadcasted_iota(jnp.int32, (8, empty.shape[1]), 0)
    edges = jnp.where(kind == 0, right, jnp.where(kind == 1, left, jnp.where(kind == 2, carry, 0.0)))

    rows = coarse.shape[0] * coarse.shape[1]
    lines = coarse[...].reshape(rows, coarse.shape[2])
    result = jnp.dot(lines, matrix[...], precision=HIGHEST) + lax.dot_general(
        edges, update[...], (((0,), (0,)), ((), ())), precision=HIGHEST
    )
    upper = result[:, :width].reshape(rows // 8, 8, width)
    lower = result[:, width:].reshape(rows // 8, 8, width)
    detail[...] = result[:, width:].reshape(detail.shape)
    top = lax.broadcasted_iota(jnp.int32, upper.shape, 1) < LINES
    tiles[0] = jnp.where(top, upper, pltpu.roll(lower, LINES, 1))
    tiles[1] = jnp.where(top, pltpu.roll(upper, LINES, 1), lower)
    eights = coarse.shape[1] // 8

    def scatter(x, carry):
        for j in range(eights):
            for half in range(2):
                block = x * (2 * eights * chunks) + step * (2 * eights) + 2 * j + half
                outgoing[placed[block]] = tiles[half, x * eights + j]
        return carry

    lax.fori_loop(0, coarse.shape[0], scatter, 0)


def deliver_kernel(n_gy, n_gz, outgoing, received, send_sem, recv_sem, own_sem):
    gy, gz = lax.axis_index("gy"), lax.axis_index("gz")
    me = gy * n_gz + gz
    shifts = [
        (dy, dz) for dy in range(n_gy) for dz in range(n_gz) if dy + dz > 0
    ]
    shifts.sort(key=lambda shift: -min(shift[0], n_gy - shift[0]))
    barrier = pltpu.get_barrier_semaphore()
    targets = []
    for dy, dz in shifts:
        there = (lax.rem(gy + dy, n_gy), lax.rem(gz + dz, n_gz))
        targets.append(there)
        pl.semaphore_signal(
            barrier, inc=1, device_id={"gy": there[0], "gz": there[1]}, device_id_type=MESH
        )
    own = pltpu.make_async_copy(outgoing.at[me], received.at[me], own_sem)
    own.start()
    pl.semaphore_wait(barrier, len(shifts))
    copies = []
    for k, there in enumerate(targets):
        copy = pltpu.make_async_remote_copy(
            src_ref=outgoing.at[there[0] * n_gz + there[1]],
            dst_ref=received.at[me],
            send_sem=send_sem.at[k],
            recv_sem=recv_sem.at[k],
            device_id={"gy": there[0], "gz": there[1]},
            device_id_type=MESH,
        )
        copy.start()
        copies.append(copy)
    own.wait()
    for copy in copies:
        copy.wait()


def local(sizes, nodes, spacing_x, spacing_z, factor_x, gain_x, factor_z, gain_z, receivers):
    n_gx, n_gy, n_gz = sizes
    length, lines, depth = nodes.shape
    half, width = length // 2, depth // 2
    coefs = coefficients(spacing_x).reshape(-1)
    coefz = lax.dynamic_slice_in_dim(
        coefficients(spacing_z), lax.axis_index("gz") * width, width, axis=1
    )
    gain_row = gain_z.reshape(1, width)
    vmem = pl.BlockSpec(memory_space=pltpu.VMEM)
    smem = pl.BlockSpec(memory_space=pltpu.SMEM)
    hbm = pl.BlockSpec(memory_space=pl.ANY)

    def exchange(nodes, coefs, factor, gain, out, left, right, send, tails, s_sem, r_sem):
        exchange_first(
            n_gx, nodes, coefs, factor, gain, out, left, right, send, tails, (s_sem, r_sem)
        )

    planes = pl.pallas_call(
        exchange,
        out_shape=jax.ShapeDtypeStruct((3, lines, depth), jnp.float32),
        in_specs=[vmem, smem, smem, smem],
        out_specs=vmem,
        scratch_shapes=[
            pltpu.VMEM((lines, depth), jnp.float32),
            pltpu.VMEM((lines, depth), jnp.float32),
            pltpu.VMEM((2, lines + 8, depth), jnp.float32),
            pltpu.VMEM((n_gx, lines + 8, depth), jnp.float32),
            pltpu.SemaphoreType.DMA((n_gx + 1,)),
            pltpu.SemaphoreType.DMA((n_gx + 1,)),
        ],
        compiler_params=pltpu.CompilerParams(
            collective_id=0, has_side_effects=True, vmem_limit_bytes=LIMIT
        ),
        name="exchange_first",
    )(nodes, coefs, factor_x, gain_x)

    chunks = 4
    rows = lines // chunks
    params = pltpu.CompilerParams(
        dimension_semantics=("arbitrary",), vmem_limit_bytes=LIMIT
    )
    detail_x, coarse_x, payload = pl.pallas_call(
        functools.partial(first_kernel, count=n_gx),
        grid=(chunks,),
        in_specs=[
            pl.BlockSpec((length, rows, depth), lambda i: (0, i, 0)),
            pl.BlockSpec((3, rows, depth), lambda i: (0, i, 0)),
            smem, smem, smem,
            pl.BlockSpec((8, width), lambda i: (0, 0)),
            pl.BlockSpec((width, width), lambda i: (0, 0)),
            pl.BlockSpec((1, width), lambda i: (0, 0)),
        ],
        out_specs=[
            pl.BlockSpec((half, rows, depth), lambda i: (0, i, 0)),
            pl.BlockSpec((half, rows, depth), lambda i: (0, i, 0)),
            pl.BlockSpec((1, 8, half * rows), lambda i: (i, 0, 0)),
        ],
        out_shape=[
            jax.ShapeDtypeStruct((half, lines, depth), jnp.float32),
            jax.ShapeDtypeStruct((half, lines, depth), jnp.float32),
            jax.ShapeDtypeStruct((chunks, 8, half * rows), jnp.float32),
        ],
        scratch_shapes=[pltpu.VMEM((8, depth), jnp.float32)],
        compiler_params=params,
        name="pass_first",
    )(nodes, planes, coefs, factor_x, gain_x, coefz, factor_z, gain_row)

    gathered = lax.all_gather(payload, "gz")

    blocks = half * lines // LINES
    group = n_gy * n_gz
    capacity = max(2, blocks // group * 2)
    targets = receivers[:, 0]
    positions = jnp.arange(blocks, dtype=jnp.int32)
    earlier = (targets[None, :] == targets[:, None]) & (positions[None, :] < positions[:, None])
    placed = targets * capacity + jnp.sum(earlier.astype(jnp.int32), axis=1)

    detail_z, outgoing = pl.pallas_call(
        functools.partial(third_kernel, count=n_gz, chunks=chunks),
        grid=(chunks,),
        in_specs=[
            smem,
            pl.BlockSpec((half, rows, depth), lambda i: (0, i, 0)),
            pl.BlockSpec((n_gz, 1, 8, half * rows), lambda i: (0, i, 0, 0)),
            pl.BlockSpec((8, width), lambda i: (0, 0)),
            pl.BlockSpec((width, width), lambda i: (0, 0)),
            pl.BlockSpec((1, width), lambda i: (0, 0)),
        ],
        out_specs=[
            pl.BlockSpec((half, rows, width), lambda i: (0, i, 0)),
            pl.BlockSpec((group * capacity, 2 * LINES, width), lambda i: (0, 0, 0)),
        ],
        out_shape=[
            jax.ShapeDtypeStruct((half, lines, width), jnp.float32),
            jax.ShapeDtypeStruct((group * capacity, 2 * LINES, width), jnp.float32),
        ],
        scratch_shapes=[
            pltpu.VMEM((depth, depth), jnp.float32),
            pltpu.VMEM((8, depth), jnp.float32),
            pltpu.VMEM((2, half * rows // 8, 8, width), jnp.float32),
        ],
        compiler_params=params,
        name="pass_third",
    )(placed, coarse_x, gathered, coefz, factor_z, gain_row)

    outgoing = outgoing.reshape(group, capacity, 2 * LINES, width)
    received = pl.pallas_call(
        functools.partial(deliver_kernel, n_gy, n_gz),
        out_shape=jax.ShapeDtypeStruct(outgoing.shape, jnp.float32),
        in_specs=[hbm],
        out_specs=hbm,
        scratch_shapes=[
            pltpu.SemaphoreType.DMA((group - 1,)),
            pltpu.SemaphoreType.DMA((group - 1,)),
            pltpu.SemaphoreType.DMA,
        ],
        compiler_params=pltpu.CompilerParams(collective_id=1, has_side_effects=True),
        name="deliver",
    )(outgoing)
    return (
        detail_x,
        detail_z,
        received.reshape(1, group, capacity, 2, LINES, width),
    )


def solution(mesh):
    sizes = tuple(mesh.shape[axis] for axis in ("gx", "gy", "gz"))
    return jax.shard_map(
        functools.partial(local, sizes),
        mesh=mesh,
        in_specs=(
            P("gx", "gy", "gz"),
            P(),
            P(),
            P("gx", None),
            P("gx"),
            P("gz", None),
            P("gz"),
            P(("gx", "gy", "gz"), None),
        ),
        out_specs=(
            P("gx", "gy", "gz"),
            P("gx", "gy", "gz"),
            P(("gx", "gy", "gz"), None, None, None, None, None),
        ),
        check_vma=False,
    )
```

time: 207 us -> 145 us (0.70)
  the two profiles are of different devices: /device:TPU:0 before, /device:TPU:15 now
where the time goes in v1:
time: 145 us; the launch traced here: 144 us
  Pallas kernels  125 us (86%)
  local copies, waits for them, and re-layouts  12.6 us (9%)
  blocking collectives  4.54 us (3%)
  other arithmetic  2.02 us (1%)
    pallas_call x1, Pallas kernels, local(): pl.pallas_call(functools.partial(deliver_kernel, n_gy, n_gz), out_shape=j...  94.3 us
    pallas_call x1, Pallas kernels, local(): pl.pallas_call(exchange, out_shape=jax.ShapeDtypeStruct((3, lines, depth)...  14.4 us
    unnamed x13, local copies, waits for them, and re-layouts  10.5 us
    pallas_call x1, Pallas kernels, local(): pl.pallas_call(functools.partial(first_kernel, count=n_gx), grid=(chunks,...  8.65 us
    pallas_call x1, Pallas kernels, local(): pl.pallas_call(functools.partial(third_kernel, count=n_gz, chunks=chunks)...  7.14 us
    all_gather x1, blocking collectives, local(): gathered = lax.all_gather(payload, 'gz')  4.54 us

profile of v1, /device:TPU:15, one launch (start us, length us, event | category | flops | bytes accessed | tf_op | source)
XLA Modules:
  0.0 144.5 jit_solution(9928146120527972165)
XLA Ops:
  0.6 0.0 copy-start.2
  0.6 0.0 copy-start.5
  0.7 1.0 convert_reduce_fusion
  1.7 0.7 multiply_add_fusion.placed
  2.3 0.8 reshape.131
  3.1 0.2 slice_reduce_fusion.3
  3.3 0.1 fusion.3
  3.4 0.1 fusion.1
  3.5 0.1 reshape.132.coefs
  3.6 0.8 reshape.133
  4.4 0.2 slice_reduce_fusion
  4.7 0.1 pad_maximum_fusion
  4.8 0.1 pad_maximum_fusion.2
  4.9 0.0 copy-start
  4.9 2.2 %copy-done = f32[32,128,256]{2,1,0:T(8,128)S(1)} copy-done((f32[32,128,256]{2,1,0:T(8,128)S(1)}, f32[32,128,256]{2,1,0:T(8,128)}, u32[]{:S(2)}) %copy-start) | copy-done | bytes 4194328
  7.1 0.0 copy-start.3
  7.1 0.7 copy-done.3
  7.8 0.0 copy-start.4
  7.8 0.7 copy-done.4
  8.4 14.4 %exchange_first.1.planes = f32[3,128,256]{2,1,0:T(8,128)S(1)} custom-call(f32[32,128,256]{2,1,0:T(8,128)S(1)} %copy-done, f32[512]{0:T(512)S(1)} %reshape.132.coefs, f32[16,16]{1,0:T(8,128)S(1)} %copy-done.3, f32[16]{0:T(128)S(1)} %copy-done.4), custom_call_target="tpu_custom_call" | custom-call | tf_op jit(solution)/shard_map/exchange_first/pallas_call | solution.py:353
  22.8 0.0 copy-done.2
  22.8 0.0 copy-done.5
  22.9 8.7 %pass_first.1 = (f32[16,128,256]{2,1,0:T(8,128)}, f32[16,128,256]{2,1,0:T(8,128)S(1)}, f32[4,8,512]{2,1,0:T(8,128)S(1)}) custom-call(f32[32,128,256]{2,1,0:T(8,128)S(1)} %copy-done, f32[3,128,256]{2,1,0:T(8,128)S(1)} %exchange_first.1.planes, f32[512]{0:T(512)S(1)} %reshape.132.coefs, f32[16,16]{1,0:T(8,128)S(1)} %copy-done.3, f32[16]{0:T(128)S(1)} %copy-done.4, ...), custom_call_target="tpu_custom_call" | custom-call | tf_op jit(solution)/shard_map/pass_first/pallas_call | solution.py:377
  31.5 4.5 %all-gather = f32[8,8,512]{2,1,0:T(8,128)S(1)} all-gather(f32[4,8,512]{2,1,0:T(8,128)S(1)} %get-tuple-element.10), channel_id=2, replica_groups=mesh['gx'=4,'gy'=4,'gz'=2] {'gz'}, dimensions={0}, use_global_device_ids=true | all-gather | bytes 196608 | tf_op jit(solution)/shard_map/all_gather | solution.py:403
  36.0 7.1 %pass_third.1 = (f32[16,128,128]{2,1,0:T(8,128)}, f32[1024,8,128]{2,1,0:T(8,128)S(1)}) custom-call(s32[512]{0:T(512)S(1)} %multiply_add_fusion.placed, f32[16,128,256]{2,1,0:T(8,128)S(1)} %get-tuple-element.9.coarse, f32[2,4,8,512]{3,2,1,0:T(8,128)S(1)} %bitcast.30, f32[8,128]{1,0:T(8,128)S(1)} %constant_dynamic-slice_fusion.coefz, ...), custom_call_target="tpu_custom_call" | custom-call | tf_op jit(solution)/shard_map/pass_third/pallas_call | solution.py:413
  43.2 0.0 copy-start.1
  43.2 2.0 %copy-done.1 = f32[1024,8,128]{2,1,0:T(8,128)} copy-done((f32[1024,8,128]{2,1,0:T(8,128)}, f32[1024,8,128]{2,1,0:T(8,128)S(1)}, u32[]{:S(2)}) %copy-start.1) | copy-done | bytes 4194328
  45.2 94.3 %deliver.1 = f32[8,128,8,128]{3,2,1,0:T(8,128)} custom-call(f32[8,128,8,128]{3,2,1,0:T(8,128)} %bitcast.29), custom_call_target="tpu_custom_call" | custom-call | tf_op jit(solution)/shard_map/deliver/pallas_call | solution.py:442
  139.5 4.9 %copy.12 = f32[1,8,128,2,4,128]{5,4,3,2,1,0:T(4,128)} copy(f32[1,8,128,2,4,128]{5,4,3,2,1,0:T(4,128)} %bitcast.33) | data formatting | bytes 8388608
  (9 shorter events, 0.1 us)
Async XLA Ops:
  0.6 22.2 %copy-start.2 = (f32[128,128]{1,0:T(8,128)S(1)}, f32[128,128]{1,0:T(8,128)}, u32[]{:S(2)}) copy-start(f32[128,128]{1,0:T(8,128)} %factor_z.3) | copy-start | bytes 196612
  0.6 22.2 %copy-start.5 = (f32[128]{0:T(128)S(1)}, f32[128]{0:T(128)}, u32[]{:S(2)}) copy-start(f32[128]{0:T(128)} %param.14) | copy-start | bytes 1540
  4.9 2.2 %copy-start = (f32[32,128,256]{2,1,0:T(8,128)S(1)}, f32[32,128,256]{2,1,0:T(8,128)}, u32[]{:S(2)}) copy-start(f32[32,128,256]{2,1,0:T(8,128)} %nodes.3) | copy-start | bytes 12582916
  7.1 0.7 copy-start.3
  7.8 0.7 copy-start.4
  43.2 2.0 %copy-start.1 = (f32[1024,8,128]{2,1,0:T(8,128)}, f32[1024,8,128]{2,1,0:T(8,128)S(1)}, u32[]{:S(2)}) copy-start(f32[1024,8,128]{2,1,0:T(8,128)S(1)} %get-tuple-element.12) | copy-start | bytes 12582916
